TPU v7x, 32 devices: a whole 2x2x4 slice. The times are simulated.
32 devices in a mesh: seq: 8 (over y, x, core), ch: 4 (over z).
Axes of the slice: x: 2, y: 2, z: 4, core: 2. Of those that a mesh axis runs over, the one named last changes fastest.
Arguments:
- inputs: bfloat16 [2048, 4096], P('seq', 'ch'), may hold values from -6 to 6
- w_value: bfloat16 [4096, 4096], P(None, 'ch'), may hold values from -0.09375 to 0.09375
- gates: bfloat16 [2, 2048, 4096], P(None, 'seq', 'ch'), may hold values from -6 to 6
- decay_rate: float32 [16, 4096], P(None, 'ch'), may hold values from 0 to 0.125, as said below
- residue: float32 [16, 4096], P(None, 'ch'), may hold values from -5 to 5
- fir_taps: float32 [128, 4096], P(None, 'ch'), may hold values from -0.5 to 0.5
- skip_gain: float32 [4096], P('ch'), may hold values from -4 to 4
Outputs:
- mixed: bfloat16 [2048, 4096], P('seq', 'ch')
Inputs may be any that keep to these rules, and one draw needn't show every extreme that they name: `decay_rate`: every rate is positive.
All inputs are finite; a program needn't handle non-finite values.
Results may differ from a plain program's by a relative error of at most 0.0049.
Values may be sent and summed in bfloat16 or wider, within the bound.
A program may use at most 384 MiB of HBM per device.

v0:
```python
import jax
import jax.numpy as jnp
from jax import lax
from jax.sharding import PartitionSpec as P


def from_behind(shard, axis, by):
    devices = lax.axis_size(axis)
    pairs = [(i, i + by) for i in range(devices) if 0 <= i + by < devices]
    return lax.ppermute(shard, axis, pairs)


def on_device(inputs, w_value, gates, decay_rate, residue, fir_taps, skip_gain):
    highest = lax.Precision.HIGHEST
    row_count = inputs.shape[0]
    chan_width = w_value.shape[1]
    tap_count = fir_taps.shape[0]
    pole_count = decay_rate.shape[0]
    block_count = row_count // tap_count
    projected = jnp.dot(
        lax.all_gather(inputs, "ch", axis=1, tiled=True),
        w_value,
        preferred_element_type=jnp.float32,
    )
    gated_value = (gates[1].astype(jnp.float32) * projected).astype(jnp.bfloat16)
    tail_rows = from_behind(gated_value[row_count - tap_count :], "seq", 1)
    blocks_b = gated_value.reshape(block_count, tap_count, chan_width)
    previous_blocks = jnp.concatenate([tail_rows[None], blocks_b[:-1]], axis=0)
    windows = jnp.concatenate([previous_blocks, blocks_b], axis=1).astype(jnp.float32)
    rates_t = decay_rate.T
    modal_coef = residue * jnp.sqrt(-jnp.expm1(-2.0 * decay_rate))
    coef_t = modal_coef.T
    lag_axis = jnp.arange(tap_count).astype(jnp.float32)
    powers = jnp.exp(-rates_t[:, :, None] * lag_axis[None, None, :])
    head_filter = jnp.einsum("cp,cpk->ck", coef_t, powers, precision=highest) + fir_taps.T
    both_filters = jnp.concatenate([head_filter, fir_taps.T], axis=1)
    row_index = jnp.arange(tap_count)
    col_index = jnp.arange(2 * tap_count)
    lag_grid = row_index[:, None] + tap_count - col_index[None, :]
    earlier_col = col_index[None, :] < tap_count
    lookup = jnp.where(earlier_col, lag_grid + tap_count, lag_grid)
    valid = jnp.where(earlier_col, lag_grid < tap_count, lag_grid >= 0)
    lookup = jnp.clip(lookup, 0, 2 * tap_count - 1)
    kernel = jnp.where(valid[None], both_filters[:, lookup], 0.0)
    conv = jnp.einsum("cij,njc->nic", kernel, windows, precision=highest)
    backward = jnp.exp(-rates_t[:, :, None] * (tap_count - 1 - lag_axis)[None, None, :])
    block_local = jnp.einsum(
        "cpj,njc->npc", backward, blocks_b.astype(jnp.float32), precision=highest
    )
    step_decay = jnp.exp(-decay_rate * tap_count)

    def advance(state, local_state):
        return (step_decay * state + local_state, state)

    section_state, block_starts = lax.scan(
        advance, jnp.zeros((pole_count, chan_width), jnp.float32), block_local
    )
    section_decay = jnp.exp(-decay_rate * row_count)

    def relay(turn, received):
        return from_behind(section_decay * received + section_state, "seq", 1)

    incoming = lax.fori_loop(
        0, lax.axis_size("seq") - 1, relay, jnp.zeros((pole_count, chan_width), jnp.float32)
    )
    block_offsets = (tap_count * jnp.arange(block_count)).astype(jnp.float32)
    block_powers = jnp.exp(-decay_rate[None, :, :] * block_offsets[:, None, None])
    states = block_starts + block_powers * incoming[None]
    outlook = coef_t[:, :, None] * jnp.exp(-rates_t[:, :, None] * (lag_axis + 1.0)[None, None, :])
    conv = conv + jnp.einsum("cpi,npc->nic", outlook, states, precision=highest)
    mixed = gates[0].astype(jnp.float32) * (
        conv.reshape(row_count, chan_width) + skip_gain * gated_value.astype(jnp.float32)
    )
    return mixed.astype(jnp.bfloat16)


def solution(mesh):
    in_specs = (
        P("seq", "ch"),
        P(None, "ch"),
        P(None, "seq", "ch"),
        P(None, "ch"),
        P(None, "ch"),
        P(None, "ch"),
        P("ch"),
    )
    out_specs = P("seq", "ch")
    return jax.shard_map(
        on_device, mesh=mesh, in_specs=in_specs, out_specs=out_specs, check_vma=False
    )
```

profile of v0, /device:TPU:4, one launch (start us, length us, event | category | flops | bytes accessed | tf_op | source)
XLA Modules:
  0.0 457.6 jit_solution(3494886758865828099)
XLA Ops:
  9.8 11.8 %multiply_reduce_fusion = f32[1024,128]{1,0:T(8,128)S(1)} fusion(f32[1024,16]{1,0:T(8,128)S(1)} %copy.28, f32[128]{0:T(128)S(1)} %iota_convert_fusion, f32[1024,16]{1,0:T(8,128)S(1)} %copy.16), kind=kLoop, calls=%fused_computation.9 | loop fusion | flops 6160384 | bytes 655872
  23.7 140.5 %gather_fusion = f32[32768,1024]{1,0:T(8,128)} fusion(f32[1024,256]{0,1:T(8,128)S(1)} %pad_maximum_fusion.1, s32[32768]{0:T(1024)S(1)} %broadcast_clamp_fusion), kind=kCustom, calls=%fused_computation | custom fusion | bytes 268566528 | tf_op jit(solution)/shard_map/gather | solution.py:44
  164.2 132.1 %copy.17 = f32[128,256,1024]{1,0,2:T(8,128)} copy(f32[128,256,1024]{2,1,0:T(8,128)} %bitcast.8) | data formatting | bytes 268435456 | tf_op jit(solution)/shard_map/gather | solution.py:44
  296.5 6.4 %fusion.26 = bf16[256,1024]{1,0:T(8,128)(2,1)S(1)} fusion(bf16[256,4096]{1,0:T(8,128)(2,1)} %all-gather.2.cloned.1.call-done, bf16[4096,1024]{1,0:T(8,128)(2,1)} %param.12, bf16[2,256,1024]{2,1,0:T(8,128)(2,1)S(1)} %copy-done.7), kind=kOutput, calls=%fused_computation.26 | convolution fusion | flops 2148270080 | bytes 11534336 | tf_op jit(solution)/shard_map/dot_general | solution.py:20
  304.1 8.1 %fusion.17 = f32[2,16,1024]{1,0,2:T(2,128)S(1)} fusion(bf16[2,128,1024]{1,0,2:T(2,128)(2,1)S(1)} %copy.19, f32[128]{0:T(128)S(1)} %broadcast_subtract_fusion, f32[1024,16]{1,0:T(8,128)S(1)} %copy-done.5), kind=kOutput, calls=%fused_computation.22 | convolution fusion | flops 52428800 | bytes 721408 | tf_op jit(solution)/shard_map/cpj,njc->npc/dot_general | solution.py:47
  312.8 2.1 collective-permute-start.1
  314.9 46.4 %while.23 = (s32[]{:T(128)}, f32[16,1024]{1,0:T(8,128)S(1)}, f32[16,1024]{1,0:T(8,128)S(1)}, f32[16,1024]{1,0:T(8,128)S(1)}, s32[]{:T(128)}) while((s32[]{:T(128)}, f32[16,1024]{1,0:T(8,128)S(1)}, f32[16,1024]{1,0:T(8,128)S(1)}, f32[16,1024]{1,0:T(8,128)S(1)}, s32[]{:T(128)}) %tuple.51), condition=%wide.region_3.4_spmd, body=%wide.region_2.3_spmd.sunk | while | flops 32770 | bytes 524389 | solution.py:63
  314.9 3.5 collective-permute-start
  318.5 3.8 collective-permute-done
  322.3 1.9 collective-permute-start
  324.2 4.6 collective-permute-done
  328.8 1.9 collective-permute-start
  330.7 4.6 collective-permute-done
  335.3 1.9 collective-permute-start
  337.2 4.6 collective-permute-done
  341.8 1.9 collective-permute-start
  343.7 4.6 collective-permute-done
  348.3 1.9 collective-permute-start
  350.2 4.6 collective-permute-done
  354.8 1.9 collective-permute-start
  356.7 4.6 collective-permute-done
  363.6 70.7 %fusion = f32[1024,2,128]{2,1,0:T(2,128)S(1)} fusion(bf16[2,256,1024]{1,0,2:T(2,128)(2,1)S(1)} %copy.18, f32[128,256,1024]{1,0,2:T(8,128)} %copy.17, pred[128,256]{1,0:T(8,128)(4,1)S(1)} %fusion.32), kind=kOutput, calls=%fused_computation.4 | convolution fusion | flops 838860800 | bytes 136347648 | tf_op jit(solution)/shard_map/cij,njc->nic/dot_general | solution.py:45
  434.3 12.8 %fusion.23 = f32[2,128,1024]{1,0,2:T(2,128)} fusion(f32[1024,2,128]{2,1,0:T(2,128)S(1)} %fusion, f32[2,16,1024]{1,0,2:T(2,128)} %copy.22, f32[1024,16]{1,0:T(8,128)} %copy-done.6, f32[128]{0:T(128)S(1)} %broadcast_add_fusion, f32[1024,16]{1,0:T(8,128)S(1)} %copy-done.5), kind=kOutput, calls=%fused_computation.24 | convolution fusion | flops 54788096 | bytes 2359808 | tf_op jit(solution)/shard_map/cpi,npc->nic/dot_general | solution.py:70
  448.7 2.1 fusion.27
  (73 shorter events, 11.1 us)
Async XLA Ops:
  6.5 17.0 %copy-start.3 = (f32[128,1024]{1,0:T(8,128)S(1)}, f32[128,1024]{1,0:T(8,128)}, u32[]{:S(2)}) copy-start(f32[128,1024]{1,0:T(8,128)} %param.16) | copy-start | bytes 1572868
  6.5 290.0 %all-gather.2.cloned.1.call-start = ((), (), s32[]{:S(2)}) async-start(), calls=%async_computation | async-start | bytes 2621440 | tf_op jit(solution)/shard_map/all_gather | solution.py:21
  9.0 0.8 copy-start.4
  9.3 14.3 %copy-start.6 = (f32[1024,16]{1,0:T(8,128)}, f32[1024,16]{1,0:T(8,128)S(1)}, u32[]{:S(2)}) copy-start(f32[1024,16]{1,0:T(8,128)S(1)} %copy.28) | copy-start | bytes 196612
  21.8 0.5 copy-start.11
  21.8 0.5 copy-start.13
  164.2 132.1 %copy-start.12 = (s32[128]{0:T(128)S(1)}, s32[128]{0:T(128)}, u32[]{:S(2)}) copy-start(s32[128]{0:T(128)} %copy-done.11) | copy-start | bytes 1540
  164.2 132.1 %copy-start.14 = (pred[256]{0:T(512)(128)(4,1)S(1)}, pred[256]{0:T(512)(128)(4,1)}, u32[]{:S(2)}) copy-start(pred[256]{0:T(512)(128)(4,1)} %copy-done.13) | copy-start | bytes 772
  164.2 132.3 %copy-start.7 = (bf16[2,256,1024]{2,1,0:T(8,128)(2,1)S(1)}, bf16[2,256,1024]{2,1,0:T(8,128)(2,1)}, u32[]{:S(2)}) copy-start(bf16[2,256,1024]{2,1,0:T(8,128)(2,1)} %param.13) | copy-start | bytes 3145732
  296.5 7.6 %copy-start.5 = (f32[1024,16]{1,0:T(8,128)S(1)}, f32[1024,16]{1,0:T(8,128)}, u32[]{:S(2)}) copy-start(f32[1024,16]{1,0:T(8,128)} %copy-done.4) | copy-start | bytes 196612
  304.1 8.5 %copy-start = (f32[16,1024]{1,0:T(8,128)S(1)}, f32[16,1024]{1,0:T(8,128)}, u32[]{:S(2)}) copy-start(f32[16,1024]{1,0:T(8,128)} %custom-call) | copy-start | bytes 196612
  304.1 8.5 %copy-start.2 = (f32[16,1024]{1,0:T(8,128)S(1)}, f32[16,1024]{1,0:T(8,128)}, u32[]{:S(2)}) copy-start(f32[16,1024]{1,0:T(8,128)} %get-tuple-element.170) | copy-start | bytes 196612
  304.1 8.5 %copy-start.9 = (f32[2,16,1024]{2,1,0:T(8,128)S(1)}, f32[2,16,1024]{2,1,0:T(8,128)}, u32[]{:S(2)}) copy-start(f32[2,16,1024]{2,1,0:T(8,128)} %custom-call.3) | copy-start | bytes 393220
  304.1 10.8 %copy-start.1 = (f32[16,1024]{1,0:T(8,128)S(1)}, f32[16,1024]{1,0:T(8,128)}, u32[]{:S(2)}) copy-start(f32[16,1024]{1,0:T(8,128)} %get-tuple-element.190) | copy-start | bytes 196612
  304.1 57.2 %copy-start.8 = (f32[16,1024]{1,0:T(8,128)S(1)}, f32[16,1024]{1,0:T(8,128)}, u32[]{:S(2)}) copy-start(f32[16,1024]{1,0:T(8,128)} %get-tuple-element.106) | copy-start | bytes 196612
  312.8 49.9 %collective-permute-start.1 = (bf16[128,1024]{1,0:T(8,128)(2,1)}, bf16[128,1024]{1,0:T(8,128)(2,1)S(1)}, u32[]{:S(2)}, u32[]{:S(2)}) collective-permute-start(bf16[128,1024]{1,0:T(8,128)(2,1)} %get-tuple-element.104), channel_id=1, source_target_pairs={{0,4},{4,8},{8,12},{12,16},{16,20},{20,24},{24,28},{1,5},{5,9},{9,... | collective-permute-start | bytes 786440 | tf_op jit(solution)/shard_map/ppermute | solution.py:10
  314.9 7.3 %collective-permute-start = (f32[16,1024]{1,0:T(8,128)S(1)}, f32[16,1024]{1,0:T(8,128)S(1)}, u32[]{:S(2)}, u32[]{:S(2)}) collective-permute-start(f32[16,1024]{1,0:T(8,128)S(1)} %multiply_add_fusion.3), channel_id=1, source_target_pairs={{0,4},{4,8},{8,12},{12,16},{16,20},{20,24},{24,28},{1,5},{5,9},{9,... | collective-permute-start | bytes 196616 | tf_op jit(solution)/shard_map/while/body/eval_jaxpr/ppermute | solution.py:10
  322.3 6.5 %collective-permute-start = (f32[16,1024]{1,0:T(8,128)S(1)}, f32[16,1024]{1,0:T(8,128)S(1)}, u32[]{:S(2)}, u32[]{:S(2)}) collective-permute-start(f32[16,1024]{1,0:T(8,128)S(1)} %multiply_add_fusion.3), channel_id=1, source_target_pairs={{0,4},{4,8},{8,12},{12,16},{16,20},{20,24},{24,28},{1,5},{5,9},{9,... | collective-permute-start | bytes 196616 | tf_op jit(solution)/shard_map/while/body/eval_jaxpr/ppermute | solution.py:10
  328.8 6.5 %collective-permute-start = (f32[16,1024]{1,0:T(8,128)S(1)}, f32[16,1024]{1,0:T(8,128)S(1)}, u32[]{:S(2)}, u32[]{:S(2)}) collective-permute-start(f32[16,1024]{1,0:T(8,128)S(1)} %multiply_add_fusion.3), channel_id=1, source_target_pairs={{0,4},{4,8},{8,12},{12,16},{16,20},{20,24},{24,28},{1,5},{5,9},{9,... | collective-permute-start | bytes 196616 | tf_op jit(solution)/shard_map/while/body/eval_jaxpr/ppermute | solution.py:10
  335.3 6.5 %collective-permute-start = (f32[16,1024]{1,0:T(8,128)S(1)}, f32[16,1024]{1,0:T(8,128)S(1)}, u32[]{:S(2)}, u32[]{:S(2)}) collective-permute-start(f32[16,1024]{1,0:T(8,128)S(1)} %multiply_add_fusion.3), channel_id=1, source_target_pairs={{0,4},{4,8},{8,12},{12,16},{16,20},{20,24},{24,28},{1,5},{5,9},{9,... | collective-permute-start | bytes 196616 | tf_op jit(solution)/shard_map/while/body/eval_jaxpr/ppermute | solution.py:10
  341.8 6.5 %collective-permute-start = (f32[16,1024]{1,0:T(8,128)S(1)}, f32[16,1024]{1,0:T(8,128)S(1)}, u32[]{:S(2)}, u32[]{:S(2)}) collective-permute-start(f32[16,1024]{1,0:T(8,128)S(1)} %multiply_add_fusion.3), channel_id=1, source_target_pairs={{0,4},{4,8},{8,12},{12,16},{16,20},{20,24},{24,28},{1,5},{5,9},{9,... | collective-permute-start | bytes 196616 | tf_op jit(solution)/shard_map/while/body/eval_jaxpr/ppermute | solution.py:10
  348.3 6.5 %collective-permute-start = (f32[16,1024]{1,0:T(8,128)S(1)}, f32[16,1024]{1,0:T(8,128)S(1)}, u32[]{:S(2)}, u32[]{:S(2)}) collective-permute-start(f32[16,1024]{1,0:T(8,128)S(1)} %multiply_add_fusion.3), channel_id=1, source_target_pairs={{0,4},{4,8},{8,12},{12,16},{16,20},{20,24},{24,28},{1,5},{5,9},{9,... | collective-permute-start | bytes 196616 | tf_op jit(solution)/shard_map/while/body/eval_jaxpr/ppermute | solution.py:10
  354.8 6.5 %collective-permute-start = (f32[16,1024]{1,0:T(8,128)S(1)}, f32[16,1024]{1,0:T(8,128)S(1)}, u32[]{:S(2)}, u32[]{:S(2)}) collective-permute-start(f32[16,1024]{1,0:T(8,128)S(1)} %multiply_add_fusion.3), channel_id=1, source_target_pairs={{0,4},{4,8},{8,12},{12,16},{16,20},{20,24},{24,28},{1,5},{5,9},{9,... | collective-permute-start | bytes 196616 | tf_op jit(solution)/shard_map/while/body/eval_jaxpr/ppermute | solution.py:10
  434.3 14.3 %copy-start.10 = (f32[1024]{0:T(1024)S(1)}, f32[1024]{0:T(1024)}, u32[]{:S(2)}) copy-start(f32[1024]{0:T(1024)} %param.17) | copy-start | bytes 12292
Sparse Core Ops, SparseCore 0:
  8.9 47.1 all-gather.1
where the time goes:
time: 460 us; the launch traced here: 458 us
  local copies, waits for them, and re-layouts  279 us (61%)
  matrix products  98 us (21%)
  waiting for transfers between devices  31.9 us (7%)
  other arithmetic  17.2 us (4%)
  starting transfers between devices  17.1 us (4%)
  between operations  13.8 us (3%)
    gather x2, local copies, waits for them, and re-layouts, on_device(): kernel = jnp.where(valid[None], both_filters[:, lookup], 0.0)  273 us
    dot_general x1, matrix products, on_device(): conv = jnp.einsum('cij,njc->nic', kernel, windows, precision=highest)  70.7 us
    ppermute x8, waiting for transfers between devices, from_behind(): return lax.ppermute(shard, axis, pairs)  31.1 us
    ppermute x8, starting transfers between devices, from_behind(): return lax.ppermute(shard, axis, pairs)  17.1 us
    dot_general x1, matrix products, on_device(): conv = conv + jnp.einsum('cpi,npc->nic', outlook, states, precision=highest)  12.8 us
    unnamed x3, other arithmetic  11.9 us
  transfers between devices with their start and end apart: 9, of which 7 were waited for; matrix products, arithmetic and copies ran while one was open for 63% of the time, Pallas kernels for 0%

commit v1 on v0

v1 whole, which is shorter than its diff:
```python
import functools

import jax
import jax.numpy as jnp
from jax import lax
from jax.experimental import pallas as pl
from jax.experimental.pallas import tpu as pltpu
from jax.sharding import PartitionSpec as P

MESH = pl.DeviceIdType.MESH
SUB = 8
LANES = 128
TILE = 16
CHUNK = 64
f32 = jnp.float32
bf16 = jnp.bfloat16


def fused(seqs, chs, x_ref, w_ref, gates_ref, rate_ref, res_ref, fir_ref, skip_ref, out_ref,
          x_all, w_v, sig, x3, y3, f3, q3, c3, qc3, qr3, ends, tail_in, st_out, st_in, inc,
          acc, send_sem, recv_sem, w_sem, tail_sem, st_send_sem, st_recv_sem):
    rows, depth = x_ref.shape
    width = w_ref.shape[1]
    groups = width // LANES
    taps = fir_ref.shape[0]
    poles = rate_ref.shape[0]
    chunks = rows // CHUNK
    state_rows = poles * SUB
    s = lax.axis_index("seq")
    z = lax.axis_index("ch")

    def at_rows(start, size):
        return pl.ds(pl.multiple_of(start * SUB, SUB), size * SUB)

    barrier = pltpu.get_barrier_semaphore()

    def greet(other, carry):
        @pl.when(other != s)
        def _():
            pl.semaphore_signal(barrier, inc=1, device_id={"seq": other}, device_id_type=MESH)
        return carry

    lax.fori_loop(0, seqs, greet, 0)

    @pl.when(z > 0)
    def _():
        pl.semaphore_signal(barrier, inc=1, device_id={"ch": z - 1}, device_id_type=MESH)

    @pl.when(z < chs - 1)
    def _():
        pl.semaphore_signal(barrier, inc=1, device_id={"ch": z + 1}, device_id_type=MESH)

    def w_copy(origin):
        block = pl.ds(pl.multiple_of(origin * depth, depth), depth)
        return pltpu.make_async_copy(w_ref.at[block, :], w_v.at[block, :], w_sem.at[origin])

    w_copy(z).start()
    for d in range(1, chs):
        @pl.when(z - d >= 0)
        def _():
            w_copy(z - d).start()

        @pl.when(z + d <= chs - 1)
        def _():
            w_copy(z + d).start()

    neighbours = jnp.minimum(z, 1) + jnp.minimum(chs - 1 - z, 1)
    pl.semaphore_wait(barrier, seqs - 1 + neighbours)

    def chunk_rows(c):
        return pl.ds(pl.multiple_of(c * CHUNK, CHUNK), CHUNK)

    def hop(way, d, c):
        step = 1 - 2 * way
        origin = z - step * d
        src = x_ref.at[chunk_rows(c), :] if d == 0 else x_all.at[origin, chunk_rows(c), :]
        return pltpu.make_async_remote_copy(
            src_ref=src, dst_ref=x_all.at[origin, chunk_rows(c), :],
            send_sem=send_sem.at[way, d, c], recv_sem=recv_sem.at[way, d + 1, c],
            device_id={"ch": z + step}, device_id_type=MESH)

    def landed(way, d, c):
        step = 1 - 2 * way
        origin = z - step * d
        place = x_all.at[origin, chunk_rows(c), :]
        return pltpu.make_async_remote_copy(
            src_ref=place, dst_ref=place,
            send_sem=send_sem.at[way, d, c], recv_sem=recv_sem.at[way, d, c],
            device_id={"ch": z - step}, device_id_type=MESH)

    def comes(way, d):
        return z - d >= 0 if way == 0 else z + d <= chs - 1

    def goes(way):
        return z < chs - 1 if way == 0 else z > 0

    def send_own(c):
        for way in range(2):
            @pl.when(goes(way))
            def _():
                hop(way, 0, c).start()

    send_own(chunks - 1)
    send_own(chunks - 2)

    def spread(dst, first, value, count):
        for j in range(groups):
            dst[pl.ds(first * SUB + j, count, stride=SUB), :] = value[:, j * LANES:(j + 1) * LANES]

    rate = rate_ref[...]
    decay = jnp.exp(-rate)
    spread(q3, 0, decay, poles)
    spread(qc3, 0, jnp.exp(-rate * CHUNK), poles)
    spread(qr3, 0, jnp.exp(-rate * rows), poles)
    two = jnp.exp(-2.0 * rate)
    spread(c3, 0, res_ref[...] * jnp.sqrt(jnp.tanh(rate) * (1.0 + two)), poles)
    f3[0:TILE * SUB, :] = jnp.zeros((TILE * SUB, LANES), f32)
    f3[(TILE + taps) * SUB:, :] = jnp.zeros((TILE * SUB, LANES), f32)
    spread(f3, TILE, fir_ref[...], taps)
    y3[...] = jnp.zeros_like(y3)
    inc[...] = jnp.zeros_like(inc)

    def multiply(lhs, origin, first):
        for n in range(0, width, 512):
            cols = slice(n, n + 512)
            block = pl.ds(pl.multiple_of(origin * depth, depth), depth)
            product = jnp.dot(lhs, w_v[block, cols], preferred_element_type=f32)
            if first:
                acc[:, cols] = product
            else:
                acc[:, cols] += product

    def fir_tiles(first, last, low, high):
        def tile(t, carry):
            y = tuple(y3[at_rows(t * TILE + i, 1), :] for i in range(TILE))

            def step(b, y):
                xs = x3[at_rows(taps + 8 * b, 8), :]
                fs = f3[at_rows(TILE + t * TILE - 8 * b - 7, 7 + TILE), :]
                y = list(y)
                for k in range(8):
                    xk = xs[k * SUB:(k + 1) * SUB]
                    for i in range(TILE):
                        m = i - k + 7
                        y[i] = y[i] + fs[m * SUB:(m + 1) * SUB] * xk
                return tuple(y)

            y = lax.fori_loop(jnp.maximum(low, 2 * t - taps // 8),
                              jnp.minimum(high, 2 * t + 2), step, y)
            for i in range(TILE):
                y3[at_rows(t * TILE + i, 1), :] = y[i]
            return carry

        lax.fori_loop(first, last, tile, 0)

    per = CHUNK // TILE
    reach = per + taps // TILE
    tiles = rows // TILE

    def fir_chunk(c, half):
        first = c * per + half * (reach // 2)
        last = jnp.minimum(tiles, first + reach // 2)
        fir_tiles(first, last, c * (CHUNK // 8), (c + 1) * (CHUNK // 8))

    def tree(terms):
        while len(terms) > 1:
            terms = [a + b for a, b in zip(terms[::2], terms[1::2])]
        return terms[0]

    def modal_chunk(c):
        q = [q3[p * SUB:(p + 1) * SUB, :] for p in range(poles)]
        coef = [c3[p * SUB:(p + 1) * SUB, :] for p in range(poles)]

        def step(i, state):
            at = c * CHUNK + i
            x = x3[at_rows(taps + at, 1), :]
            state = tuple(q[p] * state[p] + coef[p] * x for p in range(poles))
            y3[at_rows(at, 1), :] += tree(list(state))
            return state

        zero = jnp.zeros((SUB, LANES), f32)
        state = lax.fori_loop(0, CHUNK, step, (zero,) * poles)
        ends[c] = jnp.concatenate(state, axis=0)

    def tail_copy():
        return pltpu.make_async_remote_copy(
            src_ref=sig.at[pl.ds(rows - taps, taps), :], dst_ref=tail_in,
            send_sem=tail_sem.at[0], recv_sem=tail_sem.at[1],
            device_id={"seq": s + 1}, device_id_type=MESH)

    def fir_tail():
        @pl.when(s > 0)
        def _():
            pltpu.make_async_remote_copy(
                src_ref=tail_in, dst_ref=tail_in,
                send_sem=tail_sem.at[0], recv_sem=tail_sem.at[1],
                device_id={"seq": s - 1}, device_id_type=MESH).wait_recv()
            spread(x3, 0, tail_in[...].astype(f32), taps)
            fir_tiles(0, taps // TILE, -(taps // 8), 0)

    w_copy(z).wait()

    def chunk_step(i, carry):
        c = chunks - 1 - i

        @pl.when(i + 2 < chunks)
        def _():
            send_own(c - 2)

        multiply(x_ref[chunk_rows(c), :], z, True)
        for d in range(1, chs):
            for way in range(2):
                step = 1 - 2 * way

                @pl.when(comes(way, d))
                def _():
                    landed(way, d, c).wait_recv()

                    if d < chs - 1:
                        @pl.when(goes(way))
                        def _():
                            hop(way, d, c).start()

            for way in range(2):
                step = 1 - 2 * way

                @pl.when(comes(way, d))
                def _():
                    origin = z - step * d

                    @pl.when(i == 0)
                    def _():
                        w_copy(origin).wait()
                    multiply(x_all[origin, chunk_rows(c), :], origin, False)

            @pl.when(i > 0)
            def _():
                if d == 1:
                    modal_chunk(c + 1)
                if d == min(2, chs - 1):
                    fir_chunk(c + 1, 0)
                if d == min(3, chs - 1):
                    fir_chunk(c + 1, 1)

            if d == min(2, chs - 1):
                @pl.when(i == chunks - 1)
                def _():
                    fir_tail()

        low = (gates_ref[1, chunk_rows(c), :].astype(f32) * acc[...]).astype(bf16)
        sig[chunk_rows(c), :] = low
        spread(x3, taps + c * CHUNK, low.astype(f32), CHUNK)

        @pl.when((i == taps // CHUNK - 1) & (s < seqs - 1))
        def _():
            tail_copy().start()
        return carry

    lax.fori_loop(0, chunks, chunk_step, 0)

    modal_chunk(0)
    total = ends[0]
    for c in range(1, chunks):
        total = qc3[...] * total + ends[c]
    st_out[...] = total

    def state_copy(other):
        return pltpu.make_async_remote_copy(
            src_ref=st_out, dst_ref=st_in.at[s],
            send_sem=st_send_sem.at[other], recv_sem=st_recv_sem.at[s],
            device_id={"seq": other}, device_id_type=MESH)

    def start_state(other, carry):
        state_copy(other).start()
        return carry

    lax.fori_loop(s + 1, seqs, start_state, 0)
    fir_chunk(0, 0)
    fir_chunk(0, 1)

    def take_state(other, carry):
        pltpu.make_async_remote_copy(
            src_ref=st_out, dst_ref=st_in.at[other],
            send_sem=st_send_sem.at[other], recv_sem=st_recv_sem.at[other],
            device_id={"seq": other}, device_id_type=MESH).wait_recv()
        inc[...] = qr3[...] * inc[...] + st_in[other]
        return carry

    lax.fori_loop(0, s, take_state, 0)

    q = [q3[p * SUB:(p + 1) * SUB, :] for p in range(poles)]
    for c in range(chunks):
        def step(i, state):
            at = c * CHUNK + i
            state = tuple(q[p] * state[p] for p in range(poles))
            y3[at_rows(at, 1), :] += tree(list(state))
            return state

        state = tuple(inc[p * SUB:(p + 1) * SUB, :] for p in range(poles))
        state = lax.fori_loop(0, CHUNK, step, state)
        inc[...] = jnp.concatenate(state, axis=0) + ends[c]
        part = slice(c * CHUNK, (c + 1) * CHUNK)
        for j in range(groups):
            cols = slice(j * LANES, (j + 1) * LANES)
            conv = y3[pl.ds(c * CHUNK * SUB + j, CHUNK, stride=SUB), :]
            direct = skip_ref[:, cols] * sig[part, cols].astype(f32)
            out_ref[part, cols] = (gates_ref[0, part, cols].astype(f32) * (conv + direct)).astype(bf16)

    def end_state(other, carry):
        state_copy(other).wait_send()
        return carry

    lax.fori_loop(s + 1, seqs, end_state, 0)

    @pl.when(s < seqs - 1)
    def _():
        tail_copy().wait_send()

    def end_chunk(c, carry):
        for way in range(2):
            for d in range(chs - 1):
                @pl.when(comes(way, d) & goes(way))
                def _():
                    hop(way, d, c).wait_send()
        return carry

    lax.fori_loop(0, chunks, end_chunk, 0)


def on_device(inputs, w_value, gates, decay_rate, residue, fir_taps, skip_gain):
    seqs, chs = lax.axis_size("seq"), lax.axis_size("ch")
    rows, depth = inputs.shape
    width = w_value.shape[1]
    taps = fir_taps.shape[0]
    poles = decay_rate.shape[0]
    chunks = rows // CHUNK
    state = (poles * SUB, LANES)
    vmem = pl.BlockSpec(memory_space=pltpu.VMEM)
    return pl.pallas_call(
        functools.partial(fused, seqs, chs),
        out_shape=jax.ShapeDtypeStruct((rows, width), bf16),
        in_specs=[vmem, pl.BlockSpec(memory_space=pl.ANY)] + [vmem] * 5,
        out_specs=vmem,
        scratch_shapes=[
            pltpu.VMEM((chs, rows, depth), bf16),
            pltpu.VMEM(w_value.shape, bf16),
            pltpu.VMEM((rows, width), bf16),
            pltpu.VMEM(((taps + rows) * SUB, LANES), f32),
            pltpu.VMEM((rows * SUB, LANES), f32),
            pltpu.VMEM(((taps + 2 * TILE) * SUB, LANES), f32),
            pltpu.VMEM(state, f32),
            pltpu.VMEM(state, f32),
            pltpu.VMEM(state, f32),
            pltpu.VMEM(state, f32),
            pltpu.VMEM((chunks,) + state, f32),
            pltpu.VMEM((taps, width), bf16),
            pltpu.VMEM(state, f32),
            pltpu.VMEM((seqs,) + state, f32),
            pltpu.VMEM(state, f32),
            pltpu.VMEM((CHUNK, width), f32),
            pltpu.SemaphoreType.DMA((2, chs, chunks)),
            pltpu.SemaphoreType.DMA((2, chs, chunks)),
            pltpu.SemaphoreType.DMA((chs,)),
            pltpu.SemaphoreType.DMA((2,)),
            pltpu.SemaphoreType.DMA((seqs,)),
            pltpu.SemaphoreType.DMA((seqs,)),
        ],
        compiler_params=pltpu.CompilerParams(
            collective_id=0, has_side_effects=True, vmem_limit_bytes=48 * 2**20),
        cost_estimate=pl.CostEstimate(
            flops=2 * rows * depth * chs * width, bytes_accessed=2 * depth * chs * width, transcendentals=0),
    )(inputs, w_value, gates, decay_rate, residue, fir_taps, skip_gain.reshape(1, width))


def solution(mesh):
    in_specs = (
        P("seq", "ch"),
        P(None, "ch"),
        P(None, "seq", "ch"),
        P(None, "ch"),
        P(None, "ch"),
        P(None, "ch"),
        P("ch"),
    )
    out_specs = P("seq", "ch")
    return jax.shard_map(
        on_device, mesh=mesh, in_specs=in_specs, out_specs=out_specs, check_vma=False
    )
```

time: 460 us -> 64.3 us (0.14)
  the two profiles are of different devices: /device:TPU:4 before, /device:TPU:7 now
where the time goes in v1:
time: 64.3 us; the launch traced here: 63.9 us
  Pallas kernels  57.5 us (89%)
  local copies, waits for them, and re-layouts  6.47 us (10%)
    pallas_call x1, Pallas kernels, on_device(): pl.pallas_call(functools.partial(fused, seqs, chs), out_shape=jax.ShapeDt...  57.5 us
    unnamed x13, local copies, waits for them, and re-layouts  6.47 us

profile of v1, /device:TPU:7, one launch (start us, length us, event | category | flops | bytes accessed | tf_op | source)
XLA Modules:
  0.0 63.9 jit_solution(6082788977033676767)
XLA Ops:
  0.0 0.0 copy-start
  0.0 1.2 %copy-done = bf16[2,256,1024]{2,1,0:T(8,128)(2,1)S(1)} copy-done((bf16[2,256,1024]{2,1,0:T(8,128)(2,1)S(1)}, bf16[2,256,1024]{2,1,0:T(8,128)(2,1)}, u32[]{:S(2)}) %copy-start) | copy-done | bytes 1048600
  1.2 0.0 copy-start.1
  1.2 1.0 %copy-done.1 = bf16[256,1024]{1,0:T(8,128)(2,1)S(1)} copy-done((bf16[256,1024]{1,0:T(8,128)(2,1)S(1)}, bf16[256,1024]{1,0:T(8,128)(2,1)}, u32[]{:S(2)}) %copy-start.1) | copy-done | bytes 524312
  2.3 0.0 copy-start.2
  2.3 1.0 %copy-done.2 = f32[128,1024]{1,0:T(8,128)S(1)} copy-done((f32[128,1024]{1,0:T(8,128)S(1)}, f32[128,1024]{1,0:T(8,128)}, u32[]{:S(2)}) %copy-start.2) | copy-done | bytes 524312
  3.3 0.0 copy-start.3
  3.3 0.8 %copy-done.3 = f32[16,1024]{1,0:T(8,128)S(1)} copy-done((f32[16,1024]{1,0:T(8,128)S(1)}, f32[16,1024]{1,0:T(8,128)}, u32[]{:S(2)}) %copy-start.3) | copy-done | bytes 65560
  4.2 0.0 copy-start.4
  4.2 0.8 %copy-done.4 = f32[16,1024]{1,0:T(8,128)S(1)} copy-done((f32[16,1024]{1,0:T(8,128)S(1)}, f32[16,1024]{1,0:T(8,128)}, u32[]{:S(2)}) %copy-start.4) | copy-done | bytes 65560
  5.0 0.0 copy-start.5
  5.0 0.7 %copy-done.5 = f32[1024]{0:T(1024)S(1)} copy-done((f32[1024]{0:T(1024)S(1)}, f32[1024]{0:T(1024)}, u32[]{:S(2)}) %copy-start.5) | copy-done | bytes 4120
  5.7 57.5 %shard_map.73 = bf16[256,1024]{1,0:T(8,128)(2,1)S(1)} custom-call(bf16[256,1024]{1,0:T(8,128)(2,1)S(1)} %copy-done.1, bf16[4096,1024]{1,0:T(8,128)(2,1)} %w_ref.1, bf16[2,256,1024]{2,1,0:T(8,128)(2,1)S(1)} %copy-done, f32[16,1024]{1,0:T(8,128)S(1)} %copy-done.3, f32[16,1024]{1,0:T(8,128)S(1)} %copy-done.4, f32[128,1024]{1,0:T(8,128)S(1)} %copy-done.2, ...), custom_call_target="tpu_custom_call" | custom-call | flops 2147483648 | bytes 8388608 | tf_op jit(solution)/shard_map/pallas_call | solution.py:339
  63.1 0.8 %copy.9 = bf16[256,1024]{1,0:T(8,128)(2,1)} copy(bf16[256,1024]{1,0:T(8,128)(2,1)S(1)} %shard_map.73) | data formatting | bytes 1048576
Async XLA Ops:
  0.0 1.2 %copy-start = (bf16[2,256,1024]{2,1,0:T(8,128)(2,1)S(1)}, bf16[2,256,1024]{2,1,0:T(8,128)(2,1)}, u32[]{:S(2)}) copy-start(bf16[2,256,1024]{2,1,0:T(8,128)(2,1)} %gates_ref.1) | copy-start | bytes 3145732
  1.2 1.0 %copy-start.1 = (bf16[256,1024]{1,0:T(8,128)(2,1)S(1)}, bf16[256,1024]{1,0:T(8,128)(2,1)}, u32[]{:S(2)}) copy-start(bf16[256,1024]{1,0:T(8,128)(2,1)} %x_ref.1) | copy-start | bytes 1572868
  2.3 1.0 %copy-start.2 = (f32[128,1024]{1,0:T(8,128)S(1)}, f32[128,1024]{1,0:T(8,128)}, u32[]{:S(2)}) copy-start(f32[128,1024]{1,0:T(8,128)} %fir_ref.1) | copy-start | bytes 1572868
  3.3 0.8 %copy-start.3 = (f32[16,1024]{1,0:T(8,128)S(1)}, f32[16,1024]{1,0:T(8,128)}, u32[]{:S(2)}) copy-start(f32[16,1024]{1,0:T(8,128)} %rate_ref.1) | copy-start | bytes 196612
  4.2 0.8 %copy-start.4 = (f32[16,1024]{1,0:T(8,128)S(1)}, f32[16,1024]{1,0:T(8,128)}, u32[]{:S(2)}) copy-start(f32[16,1024]{1,0:T(8,128)} %res_ref.1) | copy-start | bytes 196612
  5.0 0.7 %copy-start.5 = (f32[1024]{0:T(1024)S(1)}, f32[1024]{0:T(1024)}, u32[]{:S(2)}) copy-start(f32[1024]{0:T(1024)} %param.13) | copy-start | bytes 12292

commit v2 on v1

--- a/solution.py
+++ b/solution.py
@@ -16,9 +16,9 @@
 bf16 = jnp.bfloat16
 
 
-def fused(seqs, chs, x_ref, w_ref, gates_ref, rate_ref, res_ref, fir_ref, skip_ref, out_ref,
-          x_all, w_v, sig, x3, y3, f3, q3, c3, qc3, qr3, ends, tail_in, st_out, st_in, inc,
-          acc, send_sem, recv_sem, w_sem, tail_sem, st_send_sem, st_recv_sem):
+def fused(seqs, chs, x_ref, w_ref, gates_hbm, rate_hbm, res_hbm, fir_hbm, skip_hbm, out_ref,
+          gates_ref, rate_ref, res_ref, fir_ref, skip_ref, x_all, w_v, sig, x3, y3, f3, q3, c3, qc3, qr3, ends, tail_in, st_out, st_in, inc,
+          acc, send_sem, recv_sem, w_sem, load_sem, tail_sem, st_send_sem, st_recv_sem):
     rows, depth = x_ref.shape
     width = w_ref.shape[1]
     groups = width // LANES
@@ -54,6 +54,11 @@
         block = pl.ds(pl.multiple_of(origin * depth, depth), depth)
         return pltpu.make_async_copy(w_ref.at[block, :], w_v.at[block, :], w_sem.at[origin])
 
+    pairs = ((rate_hbm, rate_ref), (res_hbm, res_ref), (fir_hbm, fir_ref), (skip_hbm, skip_ref),
+             (x_ref, x_all.at[z]), (gates_hbm, gates_ref))
+    loads = [pltpu.make_async_copy(src, dst, load_sem.at[n]) for n, (src, dst) in enumerate(pairs)]
+    for load in loads:
+        load.start()
     w_copy(z).start()
     for d in range(1, chs):
         @pl.when(z - d >= 0)
@@ -107,6 +112,8 @@
         for j in range(groups):
             dst[pl.ds(first * SUB + j, count, stride=SUB), :] = value[:, j * LANES:(j + 1) * LANES]
 
+    for load in loads[:4]:
+        load.wait()
     rate = rate_ref[...]
     decay = jnp.exp(-rate)
     spread(q3, 0, decay, poles)
@@ -198,6 +205,8 @@
             spread(x3, 0, tail_in[...].astype(f32), taps)
             fir_tiles(0, taps // TILE, -(taps // 8), 0)
 
+    for load in loads[4:]:
+        load.wait()
     w_copy(z).wait()
 
     def chunk_step(i, carry):
@@ -207,7 +216,7 @@
         def _():
             send_own(c - 2)
 
-        multiply(x_ref[chunk_rows(c), :], z, True)
+        multiply(x_all[z, chunk_rows(c), :], z, True)
         for d in range(1, chs):
             for way in range(2):
                 step = 1 - 2 * way
@@ -339,9 +348,14 @@
     return pl.pallas_call(
         functools.partial(fused, seqs, chs),
         out_shape=jax.ShapeDtypeStruct((rows, width), bf16),
-        in_specs=[vmem, pl.BlockSpec(memory_space=pl.ANY)] + [vmem] * 5,
+        in_specs=[pl.BlockSpec(memory_space=pltpu.HBM)] * 7,
         out_specs=vmem,
         scratch_shapes=[
+            pltpu.VMEM(gates.shape, bf16),
+            pltpu.VMEM(decay_rate.shape, f32),
+            pltpu.VMEM(residue.shape, f32),
+            pltpu.VMEM(fir_taps.shape, f32),
+            pltpu.VMEM((1, width), f32),
             pltpu.VMEM((chs, rows, depth), bf16),
             pltpu.VMEM(w_value.shape, bf16),
             pltpu.VMEM((rows, width), bf16),
@@ -361,6 +375,7 @@
             pltpu.SemaphoreType.DMA((2, chs, chunks)),
             pltpu.SemaphoreType.DMA((2, chs, chunks)),
             pltpu.SemaphoreType.DMA((chs,)),
+            pltpu.SemaphoreType.DMA((6,)),
             pltpu.SemaphoreType.DMA((2,)),
             pltpu.SemaphoreType.DMA((seqs,)),
             pltpu.SemaphoreType.DMA((seqs,)),

time: 64.3 us -> 64.4 us (level)
  no operation moved by 1% of the time
where the time goes in v2:
time: 64.4 us; the launch traced here: 64 us
  Pallas kernels  57.5 us (89%)
  local copies, waits for them, and re-layouts  6.47 us (10%)
    pallas_call x1, Pallas kernels, on_device(): pl.pallas_call(functools.partial(fused, seqs, chs), out_shape=jax.ShapeDt...  57.5 us
    unnamed x13, local copies, waits for them, and re-layouts  6.47 us

profile of v2, /device:TPU:7, one launch (start us, length us, event | category | flops | bytes accessed | tf_op | source)
XLA Modules:
  0.0 64.0 jit_solution(18250816358141918348)
XLA Ops:
  0.0 0.0 copy-start
  0.0 1.2 %copy-done = bf16[2,256,1024]{2,1,0:T(8,128)(2,1)S(1)} copy-done((bf16[2,256,1024]{2,1,0:T(8,128)(2,1)S(1)}, bf16[2,256,1024]{2,1,0:T(8,128)(2,1)}, u32[]{:S(2)}) %copy-start) | copy-done | bytes 1048600
  1.2 0.0 copy-start.1
  1.2 1.0 %copy-done.1 = bf16[256,1024]{1,0:T(8,128)(2,1)S(1)} copy-done((bf16[256,1024]{1,0:T(8,128)(2,1)S(1)}, bf16[256,1024]{1,0:T(8,128)(2,1)}, u32[]{:S(2)}) %copy-start.1) | copy-done | bytes 524312
  2.3 0.0 copy-start.2
  2.3 1.0 %copy-done.2 = f32[128,1024]{1,0:T(8,128)S(1)} copy-done((f32[128,1024]{1,0:T(8,128)S(1)}, f32[128,1024]{1,0:T(8,128)}, u32[]{:S(2)}) %copy-start.2) | copy-done | bytes 524312
  3.3 0.0 copy-start.3
  3.3 0.8 %copy-done.3 = f32[16,1024]{1,0:T(8,128)S(1)} copy-done((f32[16,1024]{1,0:T(8,128)S(1)}, f32[16,1024]{1,0:T(8,128)}, u32[]{:S(2)}) %copy-start.3) | copy-done | bytes 65560
  4.2 0.0 copy-start.4
  4.2 0.8 %copy-done.4 = f32[16,1024]{1,0:T(8,128)S(1)} copy-done((f32[16,1024]{1,0:T(8,128)S(1)}, f32[16,1024]{1,0:T(8,128)}, u32[]{:S(2)}) %copy-start.4) | copy-done | bytes 65560
  5.0 0.0 copy-start.5
  5.0 0.7 %copy-done.5 = f32[1024]{0:T(1024)S(1)} copy-done((f32[1024]{0:T(1024)S(1)}, f32[1024]{0:T(1024)}, u32[]{:S(2)}) %copy-start.5) | copy-done | bytes 4120
  5.7 57.5 %shard_map.73 = bf16[256,1024]{1,0:T(8,128)(2,1)S(1)} custom-call(bf16[256,1024]{1,0:T(8,128)(2,1)S(1)} %copy-done.1, bf16[4096,1024]{1,0:T(8,128)(2,1)} %w_ref.1, bf16[2,256,1024]{2,1,0:T(8,128)(2,1)S(1)} %copy-done, f32[16,1024]{1,0:T(8,128)S(1)} %copy-done.3, f32[16,1024]{1,0:T(8,128)S(1)} %copy-done.4, f32[128,1024]{1,0:T(8,128)S(1)} %copy-done.2, ...), custom_call_target="tpu_custom_call" | custom-call | flops 2147483648 | bytes 8388608 | tf_op jit(solution)/shard_map/pallas_call | solution.py:348
  63.2 0.8 %copy.9 = bf16[256,1024]{1,0:T(8,128)(2,1)} copy(bf16[256,1024]{1,0:T(8,128)(2,1)S(1)} %shard_map.73) | data formatting | bytes 1048576
Async XLA Ops:
  0.0 1.2 %copy-start = (bf16[2,256,1024]{2,1,0:T(8,128)(2,1)S(1)}, bf16[2,256,1024]{2,1,0:T(8,128)(2,1)}, u32[]{:S(2)}) copy-start(bf16[2,256,1024]{2,1,0:T(8,128)(2,1)} %gates_hbm.1) | copy-start | bytes 3145732
  1.2 1.0 %copy-start.1 = (bf16[256,1024]{1,0:T(8,128)(2,1)S(1)}, bf16[256,1024]{1,0:T(8,128)(2,1)}, u32[]{:S(2)}) copy-start(bf16[256,1024]{1,0:T(8,128)(2,1)} %x_ref.1) | copy-start | bytes 1572868
  2.3 1.0 %copy-start.2 = (f32[128,1024]{1,0:T(8,128)S(1)}, f32[128,1024]{1,0:T(8,128)}, u32[]{:S(2)}) copy-start(f32[128,1024]{1,0:T(8,128)} %fir_hbm.1) | copy-start | bytes 1572868
  3.3 0.8 %copy-start.3 = (f32[16,1024]{1,0:T(8,128)S(1)}, f32[16,1024]{1,0:T(8,128)}, u32[]{:S(2)}) copy-start(f32[16,1024]{1,0:T(8,128)} %rate_hbm.1) | copy-start | bytes 196612
  4.2 0.8 %copy-start.4 = (f32[16,1024]{1,0:T(8,128)S(1)}, f32[16,1024]{1,0:T(8,128)}, u32[]{:S(2)}) copy-start(f32[16,1024]{1,0:T(8,128)} %res_hbm.1) | copy-start | bytes 196612
  5.0 0.7 %copy-start.5 = (f32[1024]{0:T(1024)S(1)}, f32[1024]{0:T(1024)}, u32[]{:S(2)}) copy-start(f32[1024]{0:T(1024)} %param.13) | copy-start | bytes 12292

commit v3 on v2

--- a/solution.py
+++ b/solution.py
@@ -17,8 +17,8 @@
 
 
 def fused(seqs, chs, x_ref, w_ref, gates_hbm, rate_hbm, res_hbm, fir_hbm, skip_hbm, out_ref,
-          gates_ref, rate_ref, res_ref, fir_ref, skip_ref, x_all, w_v, sig, x3, y3, f3, q3, c3, qc3, qr3, ends, tail_in, st_out, st_in, inc,
-          acc, send_sem, recv_sem, w_sem, load_sem, tail_sem, st_send_sem, st_recv_sem):
+          gates_ref, rate_ref, res_ref, fir_ref, skip_ref, x_all, w_v, sig, x3, y3, f3, q3, c3, qc3, qr3, ends, tail_in, st_out, st_mate, st_in, inc, out_v,
+          acc, send_sem, recv_sem, w_sem, load_sem, tail_sem, mate_sem, st_send_sem, st_recv_sem, out_sem):
     rows, depth = x_ref.shape
     width = w_ref.shape[1]
     groups = width // LANES
@@ -35,7 +35,8 @@
     barrier = pltpu.get_barrier_semaphore()
 
     def greet(other, carry):
-        @pl.when(other != s)
+        same = (other - s) * (other - s)
+        @pl.when((same > 0) & ((lax.rem(same, 2) == 0) | (same == 1)))
         def _():
             pl.semaphore_signal(barrier, inc=1, device_id={"seq": other}, device_id_type=MESH)
         return carry
@@ -70,7 +71,8 @@
             w_copy(z + d).start()
 
     neighbours = jnp.minimum(z, 1) + jnp.minimum(chs - 1 - z, 1)
-    pl.semaphore_wait(barrier, seqs - 1 + neighbours)
+    beside = jnp.minimum(s, 1) + jnp.minimum(seqs - 1 - s, 1)
+    pl.semaphore_wait(barrier, seqs // 2 - 1 + beside + neighbours)
 
     def chunk_rows(c):
         return pl.ds(pl.multiple_of(c * CHUNK, CHUNK), CHUNK)
@@ -106,7 +108,6 @@
                 hop(way, 0, c).start()
 
     send_own(chunks - 1)
-    send_own(chunks - 2)
 
     def spread(dst, first, value, count):
         for j in range(groups):
@@ -209,40 +210,18 @@
         load.wait()
     w_copy(z).wait()
 
+    at_end = (z == 0) | (z == chs - 1)
+
     def chunk_step(i, carry):
         c = chunks - 1 - i
 
-        @pl.when(i + 2 < chunks)
-        def _():
-            send_own(c - 2)
+        @pl.when(i + 1 < chunks)
+        def _():
+            send_own(c - 1)
 
         multiply(x_all[z, chunk_rows(c), :], z, True)
         for d in range(1, chs):
-            for way in range(2):
-                step = 1 - 2 * way
-
-                @pl.when(comes(way, d))
-                def _():
-                    landed(way, d, c).wait_recv()
-
-                    if d < chs - 1:
-                        @pl.when(goes(way))
-                        def _():
-                            hop(way, d, c).start()
-
-            for way in range(2):
-                step = 1 - 2 * way
-
-                @pl.when(comes(way, d))
-                def _():
-                    origin = z - step * d
-
-                    @pl.when(i == 0)
-                    def _():
-                        w_copy(origin).wait()
-                    multiply(x_all[origin, chunk_rows(c), :], origin, False)
-
-            @pl.when(i > 0)
+            @pl.when((i > 0) & (at_end | (i < chunks - 1)))
             def _():
                 if d == 1:
                     modal_chunk(c + 1)
@@ -251,10 +230,41 @@
                 if d == min(3, chs - 1):
                     fir_chunk(c + 1, 1)
 
-            if d == min(2, chs - 1):
-                @pl.when(i == chunks - 1)
+            if d == chs - 1:
+                @pl.when((i == chunks - 1) & at_end)
                 def _():
                     fir_tail()
+
+            for way in range(2):
+                step = 1 - 2 * way
+
+                @pl.when(comes(way, d))
+                def _():
+                    landed(way, d, c).wait_recv()
+
+                    if d < chs - 1:
+                        @pl.when(goes(way))
+                        def _():
+                            hop(way, d, c).start()
+
+            for way in range(2):
+                step = 1 - 2 * way
+
+                @pl.when(comes(way, d))
+                def _():
+                    origin = z - step * d
+
+                    @pl.when(i == 0)
+                    def _():
+                        w_copy(origin).wait()
+                    multiply(x_all[origin, chunk_rows(c), :], origin, False)
+
+        @pl.when((i == chunks - 1) & jnp.logical_not(at_end))
+        def _():
+            modal_chunk(c + 1)
+            fir_chunk(c + 1, 0)
+            fir_chunk(c + 1, 1)
+            fir_tail()
 
         low = (gates_ref[1, chunk_rows(c), :].astype(f32) * acc[...]).astype(bf16)
         sig[chunk_rows(c), :] = low
@@ -271,31 +281,58 @@
     total = ends[0]
     for c in range(1, chunks):
         total = qc3[...] * total + ends[c]
-    st_out[...] = total
+    st_out[0] = total
+
+    odd = lax.rem(s, 2)
+    pair = s // 2
+    pairs_count = seqs // 2
+    partner = s + 1 - 2 * odd
+    swap = pltpu.make_async_remote_copy(
+        src_ref=st_out.at[0], dst_ref=st_mate,
+        send_sem=mate_sem.at[0], recv_sem=mate_sem.at[1],
+        device_id={"seq": partner}, device_id_type=MESH)
+    swap.start()
+    fir_chunk(0, 0)
+    swap.wait_recv()
+
+    @pl.when(odd == 0)
+    def _():
+        st_out[1] = qr3[...] * st_out[0] + st_mate[...]
+
+    @pl.when(odd == 1)
+    def _():
+        st_out[1] = qr3[...] * st_mate[...] + st_out[0]
 
     def state_copy(other):
         return pltpu.make_async_remote_copy(
-            src_ref=st_out, dst_ref=st_in.at[s],
-            send_sem=st_send_sem.at[other], recv_sem=st_recv_sem.at[s],
-            device_id={"seq": other}, device_id_type=MESH)
-
-    def start_state(other, carry):
-        state_copy(other).start()
-        return carry
-
-    lax.fori_loop(s + 1, seqs, start_state, 0)
-    fir_chunk(0, 0)
+            src_ref=st_out.at[1], dst_ref=st_in.at[pair],
+            send_sem=st_send_sem.at[other], recv_sem=st_recv_sem.at[pair],
+            device_id={"seq": 2 * other + odd}, device_id_type=MESH)
+
+    def start_state(n, carry):
+        state_copy(pairs_count + pair - n).start()
+        return carry
+
+    lax.fori_loop(pair + 1, pairs_count, start_state, 0)
     fir_chunk(0, 1)
 
     def take_state(other, carry):
         pltpu.make_async_remote_copy(
-            src_ref=st_out, dst_ref=st_in.at[other],
+            src_ref=st_out.at[1], dst_ref=st_in.at[other],
             send_sem=st_send_sem.at[other], recv_sem=st_recv_sem.at[other],
-            device_id={"seq": other}, device_id_type=MESH).wait_recv()
-        inc[...] = qr3[...] * inc[...] + st_in[other]
-        return carry
-
-    lax.fori_loop(0, s, take_state, 0)
+            device_id={"seq": 2 * other + odd}, device_id_type=MESH).wait_recv()
+        inc[...] = qr3[...] * (qr3[...] * inc[...]) + st_in[other]
+        return carry
+
+    lax.fori_loop(0, pair, take_state, 0)
+
+    @pl.when(odd == 1)
+    def _():
+        inc[...] = qr3[...] * inc[...] + st_mate[...]
+
+    def out_copy(c):
+        part = slice(c * CHUNK, (c + 1) * CHUNK)
+        return pltpu.make_async_copy(out_v.at[part, :], out_ref.at[part, :], out_sem.at[c])
 
     q = [q3[p * SUB:(p + 1) * SUB, :] for p in range(poles)]
     for c in range(chunks):
@@ -313,13 +350,15 @@
             cols = slice(j * LANES, (j + 1) * LANES)
             conv = y3[pl.ds(c * CHUNK * SUB + j, CHUNK, stride=SUB), :]
             direct = skip_ref[:, cols] * sig[part, cols].astype(f32)
-            out_ref[part, cols] = (gates_ref[0, part, cols].astype(f32) * (conv + direct)).astype(bf16)
+            out_v[part, cols] = (gates_ref[0, part, cols].astype(f32) * (conv + direct)).astype(bf16)
+        out_copy(c).start()
 
     def end_state(other, carry):
         state_copy(other).wait_send()
         return carry
 
-    lax.fori_loop(s + 1, seqs, end_state, 0)
+    lax.fori_loop(pair + 1, pairs_count, end_state, 0)
+    swap.wait_send()
 
     @pl.when(s < seqs - 1)
     def _():
@@ -334,6 +373,8 @@
         return carry
 
     lax.fori_loop(0, chunks, end_chunk, 0)
+    for c in range(chunks):
+        out_copy(c).wait()
 
 
 def on_device(inputs, w_value, gates, decay_rate, residue, fir_taps, skip_gain):
@@ -344,12 +385,11 @@
     poles = decay_rate.shape[0]
     chunks = rows // CHUNK
     state = (poles * SUB, LANES)
-    vmem = pl.BlockSpec(memory_space=pltpu.VMEM)
     return pl.pallas_call(
         functools.partial(fused, seqs, chs),
         out_shape=jax.ShapeDtypeStruct((rows, width), bf16),
         in_specs=[pl.BlockSpec(memory_space=pltpu.HBM)] * 7,
-        out_specs=vmem,
+        out_specs=pl.BlockSpec(memory_space=pltpu.HBM),
         scratch_shapes=[
             pltpu.VMEM(gates.shape, bf16),
             pltpu.VMEM(decay_rate.shape, f32),
@@ -368,20 +408,24 @@
             pltpu.VMEM(state, f32),
             pltpu.VMEM((chunks,) + state, f32),
             pltpu.VMEM((taps, width), bf16),
-            pltpu.VMEM(state, f32),
-            pltpu.VMEM((seqs,) + state, f32),
-            pltpu.VMEM(state, f32),
+            pltpu.VMEM((2,) + state, f32),
+            pltpu.VMEM(state, f32),
+            pltpu.VMEM((seqs // 2,) + state, f32),
+            pltpu.VMEM(state, f32),
+            pltpu.VMEM((rows, width), bf16),
             pltpu.VMEM((CHUNK, width), f32),
             pltpu.SemaphoreType.DMA((2, chs, chunks)),
             pltpu.SemaphoreType.DMA((2, chs, chunks)),
             pltpu.SemaphoreType.DMA((chs,)),
             pltpu.SemaphoreType.DMA((6,)),
             pltpu.SemaphoreType.DMA((2,)),
-            pltpu.SemaphoreType.DMA((seqs,)),
-            pltpu.SemaphoreType.DMA((seqs,)),
+            pltpu.SemaphoreType.DMA((2,)),
+            pltpu.SemaphoreType.DMA((seqs // 2,)),
+            pltpu.SemaphoreType.DMA((seqs // 2,)),
+            pltpu.SemaphoreType.DMA((chunks,)),
         ],
         compiler_params=pltpu.CompilerParams(
-            collective_id=0, has_side_effects=True, vmem_limit_bytes=48 * 2**20),
+            collective_id=0, has_side_effects=True, vmem_limit_bytes=63 * 2**20),
         cost_estimate=pl.CostEstimate(
             flops=2 * rows * depth * chs * width, bytes_accessed=2 * depth * chs * width, transcendentals=0),
     )(inputs, w_value, gates, decay_rate, residue, fir_taps, skip_gain.reshape(1, width))

time: 64.4 us -> 58.4 us (0.907)
  the two profiles are of different devices: /device:TPU:7 before, /device:TPU:4 now
where the time goes in v3:
time: 58.4 us; the launch traced here: 58.2 us
  Pallas kernels  56.3 us (96%)
  local copies, waits for them, and re-layouts  1.87 us (3%)
    pallas_call x1, Pallas kernels, on_device(): pl.pallas_call(functools.partial(fused, seqs, chs), out_shape=jax.ShapeDt...  56.3 us
    unnamed x1, local copies, waits for them, and re-layouts  1.87 us

profile of v3, /device:TPU:4, one launch (start us, length us, event | category | flops | bytes accessed | tf_op | source)
XLA Modules:
  0.0 58.2 jit_solution(3242985171979807347)
XLA Ops:
  0.0 56.3 %shard_map.73 = bf16[256,1024]{1,0:T(8,128)(2,1)} custom-call(bf16[256,1024]{1,0:T(8,128)(2,1)} %x_ref.1, bf16[4096,1024]{1,0:T(8,128)(2,1)} %w_ref.1, bf16[2,256,1024]{2,1,0:T(8,128)(2,1)} %gates_hbm.1, f32[16,1024]{1,0:T(8,128)} %rate_hbm.1, f32[16,1024]{1,0:T(8,128)} %res_hbm.1, f32[128,1024]{1,0:T(8,128)} %fir_hbm.1, f32[1,1024]{1,0:T(1,128)} %bitcast.1), custom_call_target="tpu_custom_call" | custom-call | flops 2147483648 | bytes 8388608 | tf_op jit(solution)/shard_map/pallas_call | solution.py:388
  56.4 1.9 %copy.9 = bf16[256,1024]{1,0:T(8,128)(2,1)} copy(bf16[256,1024]{1,0:T(8,128)(2,1)} %shard_map.73) | data formatting | bytes 1048576

commit v4 on v3

--- a/solution.py
+++ b/solution.py
@@ -11,7 +11,7 @@
 SUB = 8
 LANES = 128
 TILE = 16
-CHUNK = 64
+CHUNK = 128
 f32 = jnp.float32
 bf16 = jnp.bfloat16
 

time: 58.4 us -> 56.7 us (0.971)
  Pallas kernels: 56.3 us -> 54.4 us
    pallas_call x1, Pallas kernels: 56.3 us -> 54.4 us  [on_device(): pl.pallas_call(functools.partial(fused, seqs, chs), out_shape=jax.ShapeDt...]
where the time goes in v4:
time: 56.7 us; the launch traced here: 56.3 us
  Pallas kernels  54.4 us (96%)
  local copies, waits for them, and re-layouts  1.87 us (3%)
    pallas_call x1, Pallas kernels, on_device(): pl.pallas_call(functools.partial(fused, seqs, chs), out_shape=jax.ShapeDt...  54.4 us
    unnamed x1, local copies, waits for them, and re-layouts  1.87 us

profile of v4, /device:TPU:4, one launch (start us, length us, event | category | flops | bytes accessed | tf_op | source)
XLA Modules:
  0.0 56.3 jit_solution(16840985450974741015)
XLA Ops:
  0.0 54.4 %shard_map.73 = bf16[256,1024]{1,0:T(8,128)(2,1)} custom-call(bf16[256,1024]{1,0:T(8,128)(2,1)} %x_ref.1, bf16[4096,1024]{1,0:T(8,128)(2,1)} %w_ref.1, bf16[2,256,1024]{2,1,0:T(8,128)(2,1)} %gates_hbm.1, f32[16,1024]{1,0:T(8,128)} %rate_hbm.1, f32[16,1024]{1,0:T(8,128)} %res_hbm.1, f32[128,1024]{1,0:T(8,128)} %fir_hbm.1, f32[1,1024]{1,0:T(1,128)} %bitcast.1), custom_call_target="tpu_custom_call" | custom-call | flops 2147483648 | bytes 8388608 | tf_op jit(solution)/shard_map/pallas_call | solution.py:388
  54.4 1.9 %copy.9 = bf16[256,1024]{1,0:T(8,128)(2,1)} copy(bf16[256,1024]{1,0:T(8,128)(2,1)} %shard_map.73) | data formatting | bytes 1048576
